TPU v7x, 512 devices: a whole 4x8x8 slice. The times are simulated.
512 devices in a mesh: row: 128 (over x, y_lo, z, core), rep: 4 (over y_hi).
Axes of the slice: x: 4, y: 8 (y_hi: 4, y_lo: 2; y = y_hi * 2 + y_lo), z: 8, core: 2. Of those that a mesh axis runs over, the one named last changes fastest.
Arguments:
- pair: bfloat16 [1024, 1024, 128], P('row', 'rep'), may hold values from -6 to 6
- cotangent: bfloat16 [1024, 1024, 128], P('row', 'rep'), may hold values from -6 to 6
- token_mask: int32 [1024], replicated, may hold values 0 or 1
- in_gain: float32 [128], replicated, may hold values from 0.1 to 1.9
- in_bias: float32 [128], replicated, may hold values from -3 to 3
- proj_weight: bfloat16 [128, 640], replicated, may hold values from -0.5 to 0.5
- out_gain: float32 [128], replicated, may hold values from 0.1 to 1.9
- out_bias: float32 [128], replicated, may hold values from -3 to 3
- out_weight: bfloat16 [128, 128], replicated, may hold values from -0.5 to 0.5
Outputs:
- update: bfloat16 [1024, 1024, 128], P('row', 'rep')
- grad_pair: bfloat16 [1024, 1024, 128], P('row', 'rep')
- grad_proj_weight: float32 [128, 640], replicated
- grad_out_weight: float32 [128, 128], replicated
- grad_in_norm: float32 [2, 128], replicated
- grad_out_norm: float32 [2, 128], replicated
All inputs are finite; a program needn't handle non-finite values.
Results may differ from a plain program's by a relative error of at most 0.0072.
Values may be sent and summed in bfloat16 or wider, within the bound.
A program may use at most 64 MiB of HBM per device.

v0:
```python
import jax
import jax.numpy as jnp
from jax import lax
from jax.sharding import PartitionSpec as P

EPSILON = 1e-05


def norm_forward(values, gain_vec, bias_vec, along):
    average = jnp.mean(values, axis=along, keepdims=True)
    centred = values - average
    inv_std = lax.rsqrt(jnp.mean(centred * centred, axis=along, keepdims=True) + EPSILON)
    normed = centred * inv_std
    return (normed * gain_vec + bias_vec, normed, inv_std)


def norm_backward(upward, normed, inv_std, gain_vec, along):
    scaled = upward * gain_vec
    return inv_std * (
        scaled
        - jnp.mean(scaled, axis=along, keepdims=True)
        - normed * jnp.mean(scaled * normed, axis=along, keepdims=True)
    )


def body(
    pair, cotangent, token_mask, in_gain, in_bias, proj_weight, out_gain, out_bias, out_weight
):
    row_count = pair.shape[0]
    col_count = pair.shape[1]
    hidden = out_weight.shape[0]
    row_start = lax.axis_index("row") * row_count
    col_start = lax.axis_index("rep") * col_count
    mask_f = token_mask.astype(jnp.float32)
    pair_mask = (
        lax.dynamic_slice_in_dim(mask_f, row_start, row_count)[:, None]
        * lax.dynamic_slice_in_dim(mask_f, col_start, col_count)[None, :]
    )
    normed_in, z_hat, z_inv = norm_forward(pair.astype(jnp.float32), in_gain, in_bias, 2)
    norm_bf = normed_in.astype(jnp.bfloat16)
    w_ab = proj_weight[:, : 4 * hidden]
    w_gate = proj_weight[:, 4 * hidden :]
    proj = jnp.einsum("ijc,cd->dij", norm_bf, w_ab, preferred_element_type=jnp.float32)
    left_value, left_gate, right_value, right_gate = jnp.split(proj, 4, axis=0)
    left_sig = jax.nn.sigmoid(left_gate)
    right_sig = jax.nn.sigmoid(right_gate)
    left = (pair_mask * left_sig * left_value).astype(jnp.bfloat16)
    right = (pair_mask * right_sig * right_value).astype(jnp.bfloat16)
    gating = jax.nn.sigmoid(
        jnp.einsum("ijc,cd->ijd", norm_bf, w_gate, preferred_element_type=jnp.float32)
    )
    left_c, right_c = (
        lax.all_to_all(left, "row", split_axis=0, concat_axis=1, tiled=True),
        lax.all_to_all(right, "row", split_axis=0, concat_axis=1, tiled=True),
    )
    right_all = lax.all_gather(right_c, "rep", axis=2, tiled=True)
    right_rows = lax.dynamic_slice_in_dim(right_all, col_start, col_count, 1)
    right_part = right_rows
    product = jnp.einsum(
        "hik,hjk->hij",
        lax.all_gather(left_c, "rep", axis=2, tiled=True),
        right_part,
        preferred_element_type=jnp.float32,
    )
    tri = lax.all_to_all(
        product.astype(jnp.bfloat16), "row", split_axis=1, concat_axis=0, tiled=True
    )
    xn, x_hat, x_inv = norm_forward(
        tri.astype(jnp.float32), out_gain[:, None, None], out_bias[:, None, None], 0
    )
    xn_bf = xn.astype(jnp.bfloat16)
    projected = jnp.einsum("hij,hc->ijc", xn_bf, out_weight, preferred_element_type=jnp.float32)
    update = (gating * projected).astype(jnp.bfloat16)
    upstream = cotangent.astype(jnp.float32)
    d_proj_out = (upstream * gating).astype(jnp.bfloat16)
    d_gate = (upstream * projected * gating * (1.0 - gating)).astype(jnp.bfloat16)
    grad_wo = jnp.einsum("hij,ijc->hc", xn_bf, d_proj_out, preferred_element_type=jnp.float32)
    d_xn = jnp.einsum("ijc,hc->hij", d_proj_out, out_weight, preferred_element_type=jnp.float32)
    grad_norm_out = jnp.stack([jnp.sum(d_xn * x_hat, axis=(1, 2)), jnp.sum(d_xn, axis=(1, 2))])
    d_tri = norm_backward(d_xn, x_hat, x_inv, out_gain[:, None, None], 0).astype(jnp.bfloat16)
    d_tri_c = lax.all_to_all(d_tri, "row", split_axis=0, concat_axis=1, tiled=True)
    block_in = lax.all_gather(d_tri_c, "rep", axis=2, tiled=True)
    right_part = right_c
    d_left_sum = jnp.einsum(
        "hij,hjk->hik", block_in, right_part, preferred_element_type=jnp.float32
    )
    right_block = jnp.einsum("hij,hik->hjk", block_in, left_c, preferred_element_type=jnp.float32)
    d_left, d_right = (
        lax.all_to_all(
            d_left_sum.astype(jnp.bfloat16), "row", split_axis=1, concat_axis=0, tiled=True
        ),
        lax.all_to_all(
            right_block.astype(jnp.bfloat16), "row", split_axis=1, concat_axis=0, tiled=True
        ),
    )
    d_lm = d_left.astype(jnp.float32) * pair_mask
    d_rm = d_right.astype(jnp.float32) * pair_mask
    d_proj = jnp.concatenate(
        [
            d_lm * left_sig,
            d_lm * left_value * left_sig * (1.0 - left_sig),
            d_rm * right_sig,
            d_rm * right_value * right_sig * (1.0 - right_sig),
        ],
        axis=0,
    ).astype(jnp.bfloat16)
    grad_wp = jnp.concatenate(
        [
            jnp.einsum("ijc,dij->cd", norm_bf, d_proj, preferred_element_type=jnp.float32),
            jnp.einsum("ijc,ijd->cd", norm_bf, d_gate, preferred_element_type=jnp.float32),
        ],
        axis=1,
    )
    d_normed = jnp.einsum(
        "dij,cd->ijc", d_proj, w_ab, preferred_element_type=jnp.float32
    ) + jnp.einsum("ijd,cd->ijc", d_gate, w_gate, preferred_element_type=jnp.float32)
    grad_norm_in = jnp.stack(
        [jnp.sum(d_normed * z_hat, axis=(0, 1)), jnp.sum(d_normed, axis=(0, 1))]
    )
    grad_pair = norm_backward(d_normed, z_hat, z_inv, in_gain, 2).astype(jnp.bfloat16)
    summed_wp, summed_wo, summed_in_norm, summed_out_norm = lax.psum(
        (grad_wp, grad_wo, grad_norm_in, grad_norm_out), ("row", "rep")
    )
    factor = 1.0 / token_mask.shape[0]
    return (
        update,
        grad_pair,
        summed_wp * factor,
        summed_wo * factor,
        summed_in_norm * factor,
        summed_out_norm * factor,
    )


def solution(mesh):
    in_specs = (P("row", "rep", None), P("row", "rep", None), P(), P(), P(), P(), P(), P(), P())
    out_specs = (P("row", "rep", None), P("row", "rep", None), P(), P(), P(), P())
    return jax.shard_map(body, mesh=mesh, in_specs=in_specs, out_specs=out_specs, check_vma=False)
```

profile of v0, /device:TPU:1, one launch (start us, length us, event | category | flops | bytes accessed | tf_op | source)
XLA Modules:
  0.0 739.2 jit_solution(16941391837125644944)
XLA Ops:
  7.2 0.7 convert_element_type.81
  8.1 1.2 convert_reduce_fusion
  9.3 1.7 fusion.40
  11.1 2.0 convolution_bitcast_fusion
  13.8 1.3 copy-done.1
  15.5 34.6 %all_to_all.63 = bf16[128,8,256]{2,1,0:T(8,128)(2,1)} all-to-all(bf16[128,8,256]{2,1,0:T(8,128)(2,1)S(1)} %copy.50), channel_id=1, replica_groups=mesh['row'=128,'rep'=4] {'row'}, dimensions={0} | all-to-all | bytes 1048576 | tf_op jit(solution)/shard_map/all_to_all | solution.py:54
  50.5 24.9 %all_to_all.64 = bf16[128,8,256]{2,1,0:T(8,128)(2,1)} all-to-all(bf16[128,8,256]{2,1,0:T(8,128)(2,1)S(1)} %copy.49), channel_id=1, replica_groups=mesh['row'=128,'rep'=4] {'row'}, dimensions={0} | all-to-all | bytes 1048576 | tf_op jit(solution)/shard_map/all_to_all | solution.py:53
  75.8 33.6 %all-gather.6.cloned.1.call-done = bf16[1,1024,1024]{2,1,0:T(8,128)(2,1)} async-done(((bf16[1,1024,256]{2,1,0:T(8,128)(2,1)}), bf16[1,1024,1024]{2,1,0:T(8,128)(2,1)}) %all-gather.6.cloned.1.call-update) | async-done | bytes 2097168 | tf_op jit(solution)/shard_map/all_gather | solution.py:56
  109.3 56.6 %all-gather.4.cloned.1.call-done = bf16[1,1024,1024]{2,1,0:T(8,128)(2,1)} async-done(((bf16[1,1024,256]{2,1,0:T(8,128)(2,1)}), bf16[1,1024,1024]{2,1,0:T(8,128)(2,1)}) %all-gather.4.cloned.1.call-update) | async-done | bytes 2097168 | tf_op jit(solution)/shard_map/all_gather | solution.py:61
  165.9 2.4 fusion.30
  168.4 0.8 copy.82
  169.7 3.8 reduce.1
  173.7 30.3 %all_to_all.65 = bf16[128,2,1024]{2,1,0:T(2,128)(2,1)S(1)} all-to-all(bf16[128,2,1024]{2,1,0:T(2,128)(2,1)S(1)} %reshape.148), channel_id=1, replica_groups=mesh['row'=128,'rep'=4] {'row'}, dimensions={0} | all-to-all | bytes 1048576 | tf_op jit(solution)/shard_map/all_to_all | solution.py:65
  205.9 0.7 fusion.63
  206.7 1.8 fusion.44
  208.5 1.0 copy-done.3
  209.5 1.2 fusion.51
  210.7 2.0 multiply_convert_fusion.4
  212.7 2.2 copy.54
  214.9 25.8 %all_to_all.66 = bf16[128,8,256]{2,1,0:T(8,128)(2,1)} all-to-all(bf16[128,8,256]{2,1,0:T(8,128)(2,1)} %copy.54), channel_id=1, replica_groups=mesh['row'=128,'rep'=4] {'row'}, dimensions={0} | all-to-all | bytes 1048576 | tf_op jit(solution)/shard_map/all_to_all | solution.py:81
  240.8 51.2 %all-gather.8.cloned.1.call-done = bf16[1,1024,1024]{2,1,0:T(8,128)(2,1)} async-done(((bf16[1,1024,256]{2,1,0:T(8,128)(2,1)}), bf16[1,1024,1024]{2,1,0:T(8,128)(2,1)}) %all-gather.8.cloned.1.call-update) | async-done | bytes 2097168 | tf_op jit(solution)/shard_map/all_gather | solution.py:82
  292.0 2.3 fusion.27
  294.3 1.8 copy.81
  296.1 4.8 reduce.2
  300.9 1.0 reshape.152
  301.8 12.8 %all-to-all-start.4 = ((bf16[128,2,1024]{2,1,0:T(2,128)(2,1)}), bf16[128,2,1024]{2,1,0:T(2,128)(2,1)S(1)}, u32[]{:S(2)}, u32[]{:S(2)}) async-start(bf16[128,2,1024]{2,1,0:T(2,128)(2,1)} %reshape.152), calls=%async_computation.4 | async-start | bytes 1048576 | tf_op jit(solution)/shard_map/all_to_all | solution.py:89
  314.9 2.4 fusion.24
  317.4 0.8 copy.80
  318.2 4.6 reduce.3
  322.8 2.1 reshape.150
  325.0 7.6 %all-to-all-done.4 = bf16[128,2,1024]{2,1,0:T(2,128)(2,1)S(1)} async-done(((bf16[128,2,1024]{2,1,0:T(2,128)(2,1)}), bf16[128,2,1024]{2,1,0:T(2,128)(2,1)S(1)}, u32[]{:S(2)}, u32[]{:S(2)}) %all-to-all-start.4) | async-done | bytes 524320 | tf_op jit(solution)/shard_map/all_to_all | solution.py:89
  332.6 7.6 %all-to-all-start.5 = ((bf16[128,2,1024]{2,1,0:T(2,128)(2,1)}), bf16[128,2,1024]{2,1,0:T(2,128)(2,1)}, u32[]{:S(2)}, u32[]{:S(2)}) async-start(bf16[128,2,1024]{2,1,0:T(2,128)(2,1)} %reshape.150), calls=%async_computation.5 | async-start | bytes 1048576 | tf_op jit(solution)/shard_map/all_to_all | solution.py:92
  340.5 2.0 convolution_bitcast_fusion.3
  342.5 1.6 convolution_bitcast_fusion.2
  344.1 1.3 fusion.65
  346.3 11.5 %all-to-all-done.5 = bf16[128,2,1024]{2,1,0:T(2,128)(2,1)} async-done(((bf16[128,2,1024]{2,1,0:T(2,128)(2,1)}), bf16[128,2,1024]{2,1,0:T(2,128)(2,1)}, u32[]{:S(2)}, u32[]{:S(2)}) %all-to-all-start.5) | async-done | bytes 524320 | tf_op jit(solution)/shard_map/all_to_all | solution.py:92
  357.9 3.6 reshape.151
  361.4 1.1 bitcast_convert_fusion
  362.5 1.6 copy.60
  364.1 2.8 multiply_convert_fusion.3
  366.9 1.1 convolution_bitcast_fusion.1
  368.1 1.3 fusion.39
  369.4 95.1 %all-reduce = (f32[2,128]{1,0:T(2,128)S(1)}, f32[2,128]{1,0:T(2,128)S(1)}) all-reduce(f32[2,128]{1,0:T(2,128)S(1)} %pad_maximum_fusion.4, f32[2,128]{1,0:T(2,128)S(1)} %pad_maximum_fusion.5), channel_id=1, replica_groups=mesh['row'=128,'rep'=4] {'row','rep'}, use_global_device_ids=true, to_apply=%region_12.0 | all-reduce | flops 512 | bytes 4096 | tf_op jit(solution)/shard_map/psum | solution.py:121
  465.1 0.7 pad_maximum_fusion.3
  465.9 2.0 fusion.38
  468.4 260.8 %all-reduce.4.cloned.1.call-done = (f32[128,640]{1,0:T(8,128)}, f32[128,128]{1,0:T(8,128)}) async-done(((f32[128,640]{1,0:T(8,128)}, f32[128,128]{1,0:T(8,128)}), (f32[128,640]{1,0:T(8,128)}, f32[128,128]{1,0:T(8,128)})) %all-reduce.4.cloned.1.call-update) | async-done | bytes 393232 | tf_op jit(solution)/shard_map/psum | solution.py:121
  729.2 1.7 broadcast_multiply_fusion
  730.9 1.5 broadcast_multiply_fusion.1
  (64 shorter events, 7.3 us)
Async XLA Ops:
  7.2 198.7 %copy-start = (bf16[128,128]{1,0:T(8,128)(2,1)S(1)}, bf16[128,128]{1,0:T(8,128)(2,1)}, u32[]{:S(2)}) copy-start(bf16[128,128]{1,0:T(8,128)(2,1)} %param.17) | copy-start | bytes 98308
  7.2 102.2 %all-gather.6.cloned.1.call-start = ((), (), s32[]{:S(2)}) async-start(), calls=%async_computation.7 | async-start | bytes 2621440 | tf_op jit(solution)/shard_map/all_gather | solution.py:56
  13.2 1.9 copy-start.1
  50.1 115.8 %all-gather.4.cloned.1.call-start = ((), (), s32[]{:S(2)}) async-start(), calls=%async_computation.6 | async-start | bytes 2621440 | tf_op jit(solution)/shard_map/all_gather | solution.py:61
  75.4 216.5 %all-gather.8.cloned.1.call-start = ((), (), s32[]{:S(2)}) async-start(), calls=%async_computation.8 | async-start | bytes 2621440 | tf_op jit(solution)/shard_map/all_gather | solution.py:82
  204.7 1.2 copy-start.11
  204.7 1.2 copy-start.12
  205.2 1.5 copy-start.2
  205.2 1.5 copy-start.5
  205.2 1.5 copy-start.10
  205.2 1.5 copy-start.13
  205.2 1.5 copy-start.14
  208.5 1.0 copy-start.3
  210.7 81.3 %copy-start.7 = (bf16[128,8,256]{2,1,0:T(8,128)(2,1)S(1)}, bf16[128,8,256]{2,1,0:T(8,128)(2,1)}, u32[]{:S(2)}) copy-start(bf16[128,8,256]{2,1,0:T(8,128)(2,1)} %all_to_all.63) | copy-start | bytes 1572868
  301.8 30.8 %all-to-all-start.4 = ((bf16[128,2,1024]{2,1,0:T(2,128)(2,1)}), bf16[128,2,1024]{2,1,0:T(2,128)(2,1)S(1)}, u32[]{:S(2)}, u32[]{:S(2)}) async-start(bf16[128,2,1024]{2,1,0:T(2,128)(2,1)} %reshape.152), calls=%async_computation.4 | async-start | bytes 1048576 | tf_op jit(solution)/shard_map/all_to_all | solution.py:89
  322.8 19.7 %copy-start.4 = (f32[8,256,128]{2,1,0:T(8,128)S(1)}, f32[8,256,128]{2,1,0:T(8,128)}, u32[]{:S(2)}) copy-start(f32[8,256,128]{2,1,0:T(8,128)} %copy-done.3) | copy-start | bytes 3145732
  332.6 25.3 %all-to-all-start.5 = ((bf16[128,2,1024]{2,1,0:T(2,128)(2,1)}), bf16[128,2,1024]{2,1,0:T(2,128)(2,1)}, u32[]{:S(2)}, u32[]{:S(2)}) async-start(bf16[128,2,1024]{2,1,0:T(2,128)(2,1)} %reshape.150), calls=%async_computation.5 | async-start | bytes 1048576 | tf_op jit(solution)/shard_map/all_to_all | solution.py:92
  340.2 389.0 %all-reduce.4.cloned.1.call-start = ((), (), s32[]{:S(2)}) async-start(), calls=%async_computation.9 | async-start | bytes 786432 | tf_op jit(solution)/shard_map/psum | solution.py:121
  340.4 2.1 copy-start.6
  340.5 3.6 copy-start.9
  366.9 1.2 copy-start.8
Sparse Core Ops, SparseCore 0:
  50.2 59.0 all-gather.5
  111.4 54.4 all-gather.3
  240.9 51.0 all-gather.7
  466.0 263.1 all-reduce.3
where the time goes:
time: 745 us; the launch traced here: 739 us
  waiting for transfers between devices  421 us (57%)
  blocking collectives  211 us (28%)
  other arithmetic  31.6 us (4%)
  starting transfers between devices  21 us (3%)
  matrix products  20.2 us (3%)
  local copies, waits for them, and re-layouts  19.8 us (3%)
  between operations  14.4 us (2%)
    psum x1, waiting for transfers between devices, body(): lax.psum((grad_wp, grad_wo, grad_norm_in, grad_norm_out), ('row', 'rep'))  261 us
    psum x1, blocking collectives, body(): lax.psum((grad_wp, grad_wo, grad_norm_in, grad_norm_out), ('row', 'rep'))  95.1 us
    all_gather x1, waiting for transfers between devices, body(): lax.all_gather(left_c, 'rep', axis=2, tiled=True)  56.6 us
    all_gather x1, waiting for transfers between devices, body(): block_in = lax.all_gather(d_tri_c, 'rep', axis=2, tiled=True)  51.2 us
    all_to_all x1, blocking collectives, body(): lax.all_to_all(right, 'row', split_axis=0, concat_axis=1, tiled=True)  34.6 us
    all_gather x1, waiting for transfers between devices, body(): right_all = lax.all_gather(right_c, 'rep', axis=2, tiled=True)  33.6 us
    all_to_all x1, blocking collectives, body(): lax.all_to_all(product.astype(jnp.bfloat16), 'row', split_axis=1, concat_...  30.3 us
    all_to_all x1, blocking collectives, body(): lax.all_to_all(d_tri, 'row', split_axis=0, concat_axis=1, tiled=True)  25.8 us
  transfers between devices with their start and end apart: 6, of which 6 were waited for; matrix products, arithmetic and copies ran while one was open for 3% of the time, Pallas kernels for 0%

commit v1 on v0

v1 whole, which is shorter than its diff:
```python
import functools
import types

import jax
import jax.numpy as jnp
from jax import lax
from jax.experimental import pallas as pl
from jax.experimental.pallas import tpu as pltpu
from jax.sharding import PartitionSpec as P

EPSILON = 1e-05
MESH = pl.DeviceIdType.MESH
NX, NY, NZ = 4, 8, 8


def coordinates():
    row, rep = lax.axis_index("row"), lax.axis_index("rep")
    return row // 32, rep * 2 + (row // 16) % 2, (row // 2) % 8, row % 2


def device_at(x, y, z, core):
    return (((x * 2 + y % 2) * 8 + z) * 2 + core, y // 2)


def remote(src, dst, send_sem, recv_sem, target):
    return pltpu.make_async_remote_copy(
        src, dst, send_sem, recv_sem, device_id=target, device_id_type=MESH
    )


def copy_to(src, dst, send_sem, recv_sem, target, me):
    same = jnp.logical_and(target[0] == me[0], target[1] == me[1])

    @pl.when(same)
    def _():
        pltpu.make_async_copy(src, dst, recv_sem).start()

    @pl.when(jnp.logical_not(same))
    def _():
        remote(src, dst, send_sem, recv_sem, target).start()


def wait_for(ref, sem):
    pltpu.make_async_copy(ref, ref, sem).wait()


def send_to_owners(send, place, send_sem, recv_sem):
    x, y, z, core = coordinates()
    me = (lax.axis_index("row"), lax.axis_index("rep"))
    sign = 1 - 2 * core

    def step(s, carry):
        dz, dy, dx = s % 8, (s // 8) % 8, s // 64
        hx = (x // 2 + dx) % 2
        ty, tz = (y + sign * dy + 8) % 8, (z + sign * dz + 8) % 8
        h = hx * 64 + ty * 8 + tz
        copy_to(send.at[h], place, send_sem, recv_sem, device_at(2 * hx, ty, tz, x // 2), me)
        return carry

    lax.fori_loop(0, 128, step, 0)


def finish_sends(send, send_sem):
    x, y, z, core = coordinates()
    keeps = jnp.logical_and(x % 2 == 0, core == x // 2)

    @pl.when(keeps)
    def _():
        wait_for(send.at[pl.ds(0, 127)], send_sem)

    @pl.when(jnp.logical_not(keeps))
    def _():
        wait_for(send, send_sem)


def aligned(start, unit):
    return pl.multiple_of(start, unit)


def unpack(slots):
    wide = slots.astype(jnp.float32)
    low, high = wide[:, :8].reshape(512, 128), wide[:, 8:].reshape(512, 128)
    return jnp.concatenate([low, high], axis=1)


def pack(block):
    low, high = block[:, :128].reshape(64, 8, 128), block[:, 128:].reshape(64, 8, 128)
    return jnp.concatenate([low, high], axis=1).astype(jnp.bfloat16).reshape(2, 32, 16, 128)


def dot(a, b, contract):
    return lax.dot_general(a, b, ((contract[0], contract[1]), ((), ())), preferred_element_type=jnp.float32)


def turn(q, sign, rep):
    return (rep + sign * q + 4) % 4


def start_hop(send, stage, part, hop_send, hop_recv):
    x, y, z, core = coordinates()
    me = (lax.axis_index("row"), lax.axis_index("rep"))
    rows = pl.ds(aligned(part * 32, 32), 32)
    for bx in range(2):
        target = device_at(2 * core + bx, y, z, x // 2)
        copy_to(send.at[bx, rows], stage.at[rows], hop_send, hop_recv.at[part], target, me)


def finish_hop(send, hop_send):
    x, y, z, core = coordinates()

    @pl.when(core == x // 2)
    def _():
        wait_for(send.at[0], hop_send)

    @pl.when(core != x // 2)
    def _():
        wait_for(send, hop_send)


def spread(stage, recv, hop_recv, send_sem, recv_sem):
    x, y, z, core = coordinates()
    rep = lax.axis_index("rep")
    me = (lax.axis_index("row"), rep)
    h = core * 64 + y * 8 + z
    sign = 1 - 2 * core

    def one_part(q, carry):
        part = turn(q, sign, rep)
        wait_for(stage.at[pl.ds(aligned(part * 32, 32), 32)], hop_recv.at[part])

        def step(s, carry):
            tc, dz, dy = (s + core) % 2, (s // 2) % 8, s // 16
            ty, tz = part * 2 + (y + dy) % 2, (z + sign * dz + 8) % 8
            place = part * 32 + (ty % 2) * 16 + tz * 2 + tc
            copy_to(stage.at[place], recv.at[h], send_sem, recv_sem, device_at(x, ty, tz, tc), me)
            return carry

        lax.fori_loop(0, 32, step, 0)
        return carry

    lax.fori_loop(0, 4, one_part, 0)


def rows_of(ref, row):
    return ref[pl.ds(row, 128, stride=16), :]


def load_row(ref, i):
    return jnp.concatenate([rows_of(ref, i), rows_of(ref, 8 + i)], axis=1)


def store_row(ref, i, value):
    ref[pl.ds(i, 128, stride=16), :] = value[:, :128]
    ref[pl.ds(8 + i, 128, stride=16), :] = value[:, 128:]


def mean0(value):
    return jnp.sum(value, axis=0, keepdims=True) * (1.0 / value.shape[0])


def standardize(value):
    centred = value - mean0(value)
    inv_std = lax.rsqrt(mean0(centred * centred) + EPSILON)
    return centred * inv_std, inv_std


def standardize_back(scaled, normed, inv_std):
    return inv_std * (scaled - mean0(scaled) - normed * mean0(scaled * normed))


def wide(column):
    return jnp.concatenate([column, column], axis=1)


NN, NT = ((1,), (0,)), ((1,), (1,))


def front_row(r, i):
    z_hat, z_inv = standardize(r.pair[i].astype(jnp.float32).T)
    r.z_hat[i] = z_hat
    r.z_inv[pl.ds(i, 1)] = z_inv
    normed = (z_hat * wide(r.in_gain[...]) + wide(r.in_bias[...])).astype(jnp.bfloat16)
    r.normed[i] = normed
    proj = dot(r.proj_t[...], normed, NN)
    mask = r.mask[pl.ds(i, 1)]
    for t, rows in ((0, r.rows_a), (1, r.rows_b)):
        value, gate = proj[t * 256 : t * 256 + 128], proj[t * 256 + 128 : t * 256 + 256]
        sig = jax.nn.sigmoid(gate)
        r.value[i, t] = value
        r.sig[i, t] = sig
        store_row(rows, i, mask * sig * value)
    r.gating[i] = jax.nn.sigmoid(proj[512:])


def middle_row(r, i):
    x_hat, x_inv = standardize(load_row(r.rows_a, i))
    gain = wide(r.out_gain[...])
    xn = (x_hat * gain + wide(r.out_bias[...])).astype(jnp.bfloat16)
    r.xn[i] = xn
    projected = dot(r.out_t[...], xn, NN)
    gating, upstream = r.gating[i], r.upstream[i]
    r.update_t[i] = gating * projected
    d_proj_out = (upstream * gating).astype(jnp.bfloat16)
    r.d_proj_out[i] = d_proj_out
    r.d_proj[i, pl.ds(512, 128)] = (upstream * projected * gating * (1.0 - gating)).astype(jnp.bfloat16)
    d_xn = dot(r.out_w[...], d_proj_out, NN)
    r.out_scale[...] += d_xn * x_hat
    r.out_shift[...] += d_xn
    store_row(r.rows_b, i, standardize_back(d_xn * gain, x_hat, x_inv))


def back_row(r, i):
    mask = r.mask[pl.ds(i, 1)]
    for t, rows in ((0, r.rows_a), (1, r.rows_b)):
        d_factor = load_row(rows, i) * mask
        value, sig = r.value[i, t], r.sig[i, t]
        r.d_proj[i, pl.ds(t * 256, 128)] = (d_factor * sig).astype(jnp.bfloat16)
        r.d_proj[i, pl.ds(t * 256 + 128, 128)] = (d_factor * value * sig * (1.0 - sig)).astype(jnp.bfloat16)
    d_proj = r.d_proj[i]
    r.part[pl.ds(0, 640)] += dot(d_proj, r.normed[i], NT)
    d_normed = dot(r.proj_w[...], d_proj, NN)
    r.d_normed[i] = d_normed
    r.in_scale[...] += d_normed * r.z_hat[i]
    r.in_shift[...] += d_normed


def grad_row(r, i):
    scaled = r.d_normed[i] * wide(r.in_gain[...])
    result = standardize_back(scaled, r.z_hat[i], r.z_inv[pl.ds(i, 1)])
    r.grad_pair[i] = result.T.astype(jnp.bfloat16)


def over_rows(function, r):
    def step(i, carry):
        function(r, i)
        return carry

    lax.fori_loop(0, 8, step, 0)


def to_f32_rows(rows, tiles):
    rows[...] = tiles.astype(jnp.float32).reshape(2048, 128)


def to_tiles(rows):
    return rows[...].astype(jnp.bfloat16).reshape(128, 16, 128)


def channel_sums(value):
    return jnp.sum((value[:, :128] + value[:, 128:]).T, axis=0, keepdims=True)


def start_factors(r):
    row, rep = lax.axis_index("row"), lax.axis_index("rep")
    over_rows(front_row, r)
    r.send_f[:, 0] = to_tiles(r.rows_a)
    r.send_f[:, 1] = to_tiles(r.rows_b)
    place = r.recv_f.at[row // 64, :, rep * 64 + row % 64]
    send_to_owners(r.send_f, place, r.sem.at[0], r.sem.at[1])


def own_product(r):
    x, y, z, core = coordinates()
    row, rep = lax.axis_index("row"), lax.axis_index("rep")
    wait_for(r.recv_f.at[core], r.sem.at[1])
    mine = r.recv_f.at[core, 1]
    swap = remote(mine, mine, r.sem.at[2], r.sem.at[3], (row + 1 - 2 * core, rep))
    swap.start()

    def build(half, k):
        rows = pl.ds(aligned(half * 512, 512), 512)
        slots = pl.ds(aligned(k * 64, 64), 64)
        r.right[k, rows] = unpack(r.recv_f[half, 1, slots]).astype(jnp.bfloat16)

    def own(k, carry):
        r.left[k] = unpack(r.recv_f[core, 0, pl.ds(aligned(k * 64, 64), 64)]).astype(jnp.bfloat16)
        build(core, k)
        return carry

    def other(k, carry):
        build(1 - core, k)
        return carry

    lax.fori_loop(0, 4, own, 0)
    swap.wait_recv()
    lax.fori_loop(0, 4, other, 0)

    def result(q, carry):
        part = turn(q, 1 - 2 * (x // 2), rep)
        rows = pl.ds(aligned(part * 256, 256), 256)
        total = dot(r.left[0], r.right[0, rows], NT)
        for k in range(1, 4):
            total += dot(r.left[k], r.right[k, rows], NT)
        r.back_p[:, pl.ds(aligned(part * 32, 32), 32)] = pack(total)
        start_hop(r.back_p, r.stage_p, part, r.sem.at[4], r.hop_p)
        return carry

    lax.fori_loop(0, 4, result, 0)
    swap.wait_send()
    left_swap(r).start()


def left_swap(r):
    row, rep = lax.axis_index("row"), lax.axis_index("rep")
    return remote(r.left, r.left_other, r.sem.at[5], r.sem.at[6], (row + 1 - 2 * (row % 2), rep))


def own_gradients(r):
    x, y, z, core = coordinates()
    row, rep = lax.axis_index("row"), lax.axis_index("rep")
    wait_for(r.recv_d, r.sem.at[8])
    crossing = remote(
        r.recv_d.at[pl.ds(aligned((1 - core) * 128, 128), 128)],
        r.cross, r.sem.at[9], r.sem.at[10], (row + 1 - 2 * core, rep),
    )
    crossing.start()

    def build(k, carry):
        r.d_own[k] = unpack(r.recv_d[pl.ds(aligned(k * 64, 64), 64)]).astype(jnp.bfloat16)
        return carry

    lax.fori_loop(0, 4, build, 0)
    for a in range(2):
        slots = pl.ds(aligned(core * 128 + a * 64, 64), 64)
        r.d_mine[a] = unpack(r.recv_d[slots]).T.astype(jnp.bfloat16)

    def for_left(part, carry):
        total = dot(r.d_own[0], r.right[part, pl.ds(0, 256)], NN)
        for k in range(1, 4):
            total += dot(r.d_own[k], r.right[part, pl.ds(k * 256, 256)], NN)
        r.back_d[:, pl.ds(aligned(part * 32, 32), 32), 0] = pack(total)
        return carry

    lax.fori_loop(0, 4, for_left, 0)
    crossing.wait_recv()
    for a in range(2):
        r.d_cross[a] = unpack(r.cross[pl.ds(a * 64, 64)]).T.astype(jnp.bfloat16)
    left_swap(r).wait()

    def for_right(q, carry):
        part = turn(q, 1 - 2 * (x // 2), rep)
        totals = [
            dot(r.d_mine[a], r.left[part], NN) + dot(r.d_cross[a], r.left_other[part], NN) for a in range(2)
        ]
        r.back_d[:, pl.ds(aligned(part * 32, 32), 32), 1] = pack(jnp.concatenate(totals, axis=0))
        start_hop(r.back_d, r.stage_d, part, r.sem.at[11], r.hop_d)
        return carry

    lax.fori_loop(0, 4, for_right, 0)
    crossing.wait_send()


def sum_over_devices(r, meanwhile):
    x, y, z, core = coordinates()
    row, rep = lax.axis_index("row"), lax.axis_index("rep")
    sibling = (row + 1 - 2 * core, rep)
    sends, recvs = r.sum_send, r.sum_recv

    def at(base, start, size):
        return base.at[pl.ds(aligned(start, 8), size)]

    first = remote(at(r.part, (1 - core) * 512, 512), r.from_core, sends.at[0], recvs.at[0], sibling)
    first.start()
    first.wait_recv()
    r.half[...] = r.part[pl.ds(aligned(core * 512, 512), 512)] + r.from_core[...]

    r.from_z[z] = r.half[pl.ds(aligned(z * 64, 64), 64)]
    for dz in range(1, NZ):
        tz = (z + dz) % NZ
        remote(
            at(r.half, tz * 64, 64), r.from_z.at[z], sends.at[1], recvs.at[1], device_at(x, y, tz, core)
        ).start()
    meanwhile()
    wait_for(r.from_z.at[pl.ds(0, NZ - 1)], recvs.at[1])
    r.z_sum[...] = jnp.sum(r.from_z[...], axis=0)

    r.from_xy[x * NY + y] = r.z_sum[pl.ds(aligned(y * 8, 8), 8)]
    for d in range(1, NX * NY):
        tx, ty = (x + d // NY) % NX, (y + d % NY) % NY
        remote(
            at(r.z_sum, ty * 8, 8), r.from_xy.at[x * NY + y], sends.at[2], recvs.at[2], device_at(tx, ty, z, core)
        ).start()
    wait_for(r.from_xy.at[pl.ds(0, NX * NY - 1)], recvs.at[2])
    r.xy_sum[...] = jnp.sum(r.from_xy[...], axis=0)

    r.y_rows[y] = r.xy_sum[...]
    for dy in range(1, NY):
        remote(
            r.xy_sum, r.y_rows.at[y], sends.at[3], recvs.at[3], device_at(x, (y + dy) % NY, z, core)
        ).start()
    wait_for(r.y_rows.at[pl.ds(0, NY - 1)], recvs.at[3])

    r.z_rows[z] = r.y_rows[...]
    for dz in range(1, NZ):
        remote(
            r.y_rows, r.z_rows.at[z], sends.at[4], recvs.at[4], device_at(x, y, (z + dz) % NZ, core)
        ).start()
    wait_for(r.z_rows.at[pl.ds(0, NZ - 1)], recvs.at[4])

    r.sums[core] = r.z_rows[...]
    last = remote(r.z_rows, r.sums.at[core], sends.at[5], recvs.at[5], sibling)
    last.start()
    last.wait()

    first.wait_send()
    wait_for(r.from_z.at[pl.ds(0, NZ - 1)], sends.at[1])
    wait_for(r.from_xy.at[pl.ds(0, NX * NY - 1)], sends.at[2])
    wait_for(r.y_rows.at[pl.ds(0, NY - 1)], sends.at[3])
    wait_for(r.z_rows.at[pl.ds(0, NZ - 1)], sends.at[4])


def step_kernel(names, *refs):
    r = types.SimpleNamespace(**dict(zip(names, refs)))
    x, y, z, core = coordinates()
    row, rep = lax.axis_index("row"), lax.axis_index("rep")
    owner = x % 2 == 0

    start_factors(r)

    def turn_cotangent(r, i):
        r.upstream[i] = r.cotangent[i].astype(jnp.float32).T

    over_rows(turn_cotangent, r)
    for name in ("part", "out_scale", "out_shift", "in_scale", "in_shift"):
        ref = getattr(r, name)
        ref[...] = jnp.zeros(ref.shape, ref.dtype)

    @pl.when(owner)
    def _():
        own_product(r)

    spread(r.stage_p, r.recv_p, r.hop_p, r.sem.at[12], r.sem.at[13])
    wait_for(r.recv_p, r.sem.at[13])

    to_f32_rows(r.rows_a, r.recv_p[...])
    over_rows(middle_row, r)
    r.send_d[...] = to_tiles(r.rows_b)
    send_to_owners(r.send_d, r.recv_d.at[rep * 64 + row % 64], r.sem.at[7], r.sem.at[8])

    def finish_update(r, i):
        r.update[i] = r.update_t[i].T.astype(jnp.bfloat16)
        r.part[pl.ds(640, 128)] += dot(r.xn[i], r.d_proj_out[i], NT)

    over_rows(finish_update, r)

    @pl.when(owner)
    def _():
        own_gradients(r)

    spread(r.stage_d, r.recv_g, r.hop_d, r.sem.at[14], r.sem.at[15])
    wait_for(r.recv_g, r.sem.at[15])

    to_f32_rows(r.rows_a, r.recv_g[:, 0])
    to_f32_rows(r.rows_b, r.recv_g[:, 1])
    over_rows(back_row, r)
    norms = [channel_sums(ref[...]) for ref in (r.in_scale, r.in_shift, r.out_scale, r.out_shift)]
    r.part[pl.ds(768, 8)] = jnp.concatenate(norms + [jnp.zeros((4, 128), jnp.float32)], axis=0)

    sum_over_devices(r, lambda: over_rows(grad_row, r))

    finish_sends(r.send_f, r.sem.at[0])
    finish_sends(r.send_d, r.sem.at[7])
    wait_for(r.stage_p.at[pl.ds(0, 127)], r.sem.at[12])
    wait_for(r.stage_d.at[pl.ds(0, 127)], r.sem.at[14])

    @pl.when(owner)
    def _():
        finish_hop(r.back_p, r.sem.at[4])
        finish_hop(r.back_d, r.sem.at[11])


VMEM = pl.BlockSpec(memory_space=pltpu.VMEM)
DMA = pltpu.SemaphoreType.DMA


def scratch():
    f32, bf16 = jnp.float32, jnp.bfloat16

    def of(dtype, *shape):
        return pltpu.VMEM(shape, dtype)

    return {
        "rows_a": of(f32, 2048, 128),
        "rows_b": of(f32, 2048, 128),
        "z_hat": of(f32, 8, 128, 256),
        "z_inv": of(f32, 8, 256),
        "normed": of(bf16, 8, 128, 256),
        "value": of(f32, 8, 2, 128, 256),
        "sig": of(f32, 8, 2, 128, 256),
        "gating": of(f32, 8, 128, 256),
        "upstream": of(f32, 8, 128, 256),
        "xn": of(bf16, 8, 128, 256),
        "update_t": of(f32, 8, 128, 256),
        "d_proj_out": of(bf16, 8, 128, 256),
        "d_proj": of(bf16, 8, 640, 256),
        "d_normed": of(f32, 8, 128, 256),
        "out_scale": of(f32, 128, 256),
        "out_shift": of(f32, 128, 256),
        "in_scale": of(f32, 128, 256),
        "in_shift": of(f32, 128, 256),
        "send_f": of(bf16, 128, 2, 16, 128),
        "recv_f": of(bf16, 2, 2, 256, 16, 128),
        "left": of(bf16, 4, 512, 256),
        "right": of(bf16, 4, 1024, 256),
        "back_p": of(bf16, 2, 128, 16, 128),
        "stage_p": of(bf16, 128, 16, 128),
        "recv_p": of(bf16, 128, 16, 128),
        "send_d": of(bf16, 128, 16, 128),
        "recv_d": of(bf16, 256, 16, 128),
        "left_other": of(bf16, 4, 512, 256),
        "cross": of(bf16, 128, 16, 128),
        "d_own": of(bf16, 4, 512, 256),
        "d_mine": of(bf16, 2, 256, 512),
        "d_cross": of(bf16, 2, 256, 512),
        "back_d": of(bf16, 2, 128, 2, 16, 128),
        "stage_d": of(bf16, 128, 2, 16, 128),
        "recv_g": of(bf16, 128, 2, 16, 128),
        "part": of(f32, 1024, 128),
        "from_core": of(f32, 512, 128),
        "half": of(f32, 512, 128),
        "from_z": of(f32, 8, 64, 128),
        "z_sum": of(f32, 64, 128),
        "from_xy": of(f32, 32, 8, 128),
        "xy_sum": of(f32, 8, 128),
        "y_rows": of(f32, 8, 8, 128),
        "z_rows": of(f32, 8, 8, 8, 128),
        "sem": DMA((16,)),
        "hop_p": DMA((4,)),
        "hop_d": DMA((4,)),
        "sum_send": DMA((6,)),
        "sum_recv": DMA((6,)),
    }


INPUTS = (
    "pair", "cotangent", "mask", "in_gain", "in_bias", "out_gain", "out_bias", "proj_w", "proj_t", "out_w", "out_t",
)
OUTPUTS = ("update", "grad_pair", "sums")


def whole_step(*args):
    extra = scratch()
    names = INPUTS + OUTPUTS + tuple(extra)
    block = jax.ShapeDtypeStruct((8, 256, 128), jnp.bfloat16)
    return pl.pallas_call(
        functools.partial(step_kernel, names),
        out_shape=(block, block, jax.ShapeDtypeStruct((2, 8, 8, 8, 128), jnp.float32)),
        in_specs=[VMEM] * len(INPUTS),
        out_specs=(VMEM,) * 3,
        scratch_shapes=list(extra.values()),
        compiler_params=pltpu.CompilerParams(has_side_effects=True, vmem_limit_bytes=56 << 20),
        name="triangle_step",
    )(*args)


def body(
    pair, cotangent, token_mask, in_gain, in_bias, proj_weight, out_gain, out_bias, out_weight
):
    row_count, col_count, channels = pair.shape
    mask_f = token_mask.astype(jnp.float32)
    rows = lax.dynamic_slice_in_dim(mask_f, lax.axis_index("row") * row_count, row_count)
    cols = lax.dynamic_slice_in_dim(mask_f, lax.axis_index("rep") * col_count, col_count)
    vectors = [
        jnp.broadcast_to(v[:, None], (channels, 128)) for v in (in_gain, in_bias, out_gain, out_bias)
    ]
    update, grad_pair, sums = whole_step(
        pair, cotangent, rows[:, None] * cols[None, :], *vectors,
        proj_weight, proj_weight.T, out_weight, out_weight.T,
    )
    total = sums.reshape(1024, 128) * (1.0 / token_mask.shape[0])
    return (update, grad_pair, total[:640].T, total[640:768], total[768:770], total[770:772])


def solution(mesh):
    in_specs = (P("row", "rep", None), P("row", "rep", None), P(), P(), P(), P(), P(), P(), P())
    out_specs = (P("row", "rep", None), P("row", "rep", None), P(), P(), P(), P())
    return jax.shard_map(body, mesh=mesh, in_specs=in_specs, out_specs=out_specs, check_vma=False)
```

time: 745 us -> 198 us (0.27)
  waiting for transfers between devices: 421 us -> 0 us
  blocking collectives: 211 us -> 0 us
  Pallas kernels: 0 us -> 186 us
  other arithmetic: 31.6 us -> 2.43 us
  starting transfers between devices: 21 us -> 0 us
  matrix products: 20.2 us -> 0 us
  between operations: 14.4 us -> 0.68 us
  local copies, waits for them, and re-layouts: 19.8 us -> 8.8 us
    psum x1 -> x0, waiting for transfers between devices: 261 us -> none  [body(): lax.psum((grad_wp, grad_wo, grad_norm_in, grad_norm_out), ('row', 'rep'))]
    pallas_call x0 -> x1, Pallas kernels: none -> 186 us  [whole_step(): pl.pallas_call(functools.partial(step_kernel, names), out_shape=(block, b...]
    all_gather x3 -> x0, waiting for transfers between devices: 141 us -> none  [the longest x1 56.6 us: body(): lax.all_gather(left_c, 'rep', axis=2, tiled=True)]
    all_to_all x4 -> x0, blocking collectives: 116 us -> none  [the longest x1 34.6 us: body(): lax.all_to_all(right, 'row', split_axis=0, concat_axis=1, tiled=True)]
    psum x1 -> x0, blocking collectives: 95.1 us -> none  [body(): lax.psum((grad_wp, grad_wo, grad_norm_in, grad_norm_out), ('row', 'rep'))]
    all_to_all x2 -> x0, starting transfers between devices: 20.4 us -> none  [the longest x1 12.8 us: body(): lax.all_to_all(d_left_sum.astype(jnp.bfloat16), 'row', split_axis=1, conc...]
    dot_general x12 -> x0, matrix products: 20.2 us -> none  [the longest x1 2.43 us: body(): jnp.einsum('hij,hik->hjk', block_in, left_c, preferred_element_type=jnp.f...]
    all_to_all x2 -> x0, waiting for transfers between devices: 19.2 us -> none  [the longest x1 11.5 us: body(): lax.all_to_all(right_block.astype(jnp.bfloat16), 'row', split_axis=1, con...]
  transfers between devices with their start and end apart: 6 -> 0, of which waited for: 6 -> 0; matrix products, arithmetic and copies ran while one was open for 3% -> 0% of each run, Pallas kernels for 0% -> 0%
where the time goes in v1:
time: 198 us
  Pallas kernels  186 us (94%)
  local copies, waits for them, and re-layouts  8.8 us (4%)
  other arithmetic  2.43 us (1%)
    pallas_call x1, Pallas kernels, whole_step(): pl.pallas_call(functools.partial(step_kernel, names), out_shape=(block, b...  186 us
    unnamed x21, local copies, waits for them, and re-layouts  4.58 us

profile of v1, /device:TPU:1, one launch (start us, length us, event | category | flops | bytes accessed | tf_op | source)
XLA Modules:
  0.0 197.6 jit_solution(5140678165276504710)
XLA Ops:
  0.6 0.0 copy-start.3
  0.6 0.7 convert_element_type.3
  1.3 0.1 dynamic_slice.6
  1.4 0.1 dynamic_slice.7
  1.5 0.0 copy-start.4
  1.5 0.0 copy-start.5
  1.5 0.7 broadcast_multiply_fusion.1.refs_2_
  2.2 0.0 copy-done.3
  2.2 0.0 copy-start
  2.2 0.7 copy.16
  2.9 0.0 copy-done.4
  2.9 0.7 broadcast_in_dim.8.refs_3_
  3.6 0.0 copy-done.5
  3.6 0.0 copy-start.6
  3.6 0.7 broadcast_in_dim.9.refs_4_
  4.3 0.0 copy-done.6
  4.3 0.0 copy-start.7
  4.3 0.7 broadcast_in_dim.10.refs_5_
  5.0 0.0 copy-done.7
  5.0 0.7 broadcast_in_dim.11.refs_6_
  5.7 0.0 copy-done
  5.7 0.8 copy.15
  6.5 185.7 %triangle_step.1 = (bf16[8,256,128]{2,1,0:T(8,128)(2,1)}, bf16[8,256,128]{2,1,0:T(8,128)(2,1)}, f32[2,8,8,8,128]{4,3,2,1,0:T(8,128)}) custom-call(bf16[8,256,128]{2,1,0:T(8,128)(2,1)} %refs_0_.1, bf16[8,256,128]{2,1,0:T(8,128)(2,1)} %refs_1_.1, f32[8,256]{1,0:T(8,128)} %broadcast_multiply_fusion.1.refs_2_, f32[128,128]{1,0:T(8,128)} %broadcast_in_dim.8.refs_3_, ...), custom_call_target="tpu_custom_call" | custom-call | tf_op jit(solution)/shard_map/triangle_step/pallas_call | solution.py:545
  192.3 1.1 broadcast_multiply_fusion
  193.4 0.6 fusion
  193.9 0.6 slice.17
  194.6 0.0 copy-start.2
  194.6 0.9 copy.17
  195.5 0.1 copy-done.2
  195.6 0.0 copy-start.1
  195.6 0.8 copy.20
  196.4 0.4 copy-done.1
  196.8 0.8 copy.21
  (1 shorter events, 0.0 us)
Async XLA Ops:
  0.6 1.5 copy-start.3
  1.5 1.4 copy-start.4
  1.5 2.1 %copy-start.5 = (f32[128]{0:T(128)S(1)}, f32[128]{0:T(128)}, u32[]{:S(2)}) copy-start(f32[128]{0:T(128)} %param.13) | copy-start | bytes 1540
  2.2 3.6 %copy-start = (bf16[128,640]{1,0:T(8,128)(2,1)S(1)}, bf16[128,640]{1,0:T(8,128)(2,1)}, u32[]{:S(2)}) copy-start(bf16[128,640]{1,0:T(8,128)(2,1)} %refs_7_.1) | copy-start | bytes 491524
  3.6 0.7 copy-start.6
  4.3 0.7 copy-start.7
  194.6 1.0 copy-start.2
  195.6 1.2 copy-start.1

commit v2 on v1

--- a/solution.py
+++ b/solution.py
@@ -44,7 +44,7 @@
     pltpu.make_async_copy(ref, ref, sem).wait()
 
 
-def send_to_owners(send, place, send_sem, recv_sem):
+def send_to_owners(send, place, send_sem, recv_sem, first=0, last=128):
     x, y, z, core = coordinates()
     me = (lax.axis_index("row"), lax.axis_index("rep"))
     sign = 1 - 2 * core
@@ -57,7 +57,7 @@
         copy_to(send.at[h], place, send_sem, recv_sem, device_at(2 * hx, ty, tz, x // 2), me)
         return carry
 
-    lax.fori_loop(0, 128, step, 0)
+    lax.fori_loop(first, last, step, 0)
 
 
 def finish_sends(send, send_sem):
@@ -173,6 +173,19 @@
 
 
 NN, NT = ((1,), (0,)), ((1,), (1,))
+
+
+def neighbours():
+    x, y, z, core = coordinates()
+    in_z = [device_at(x, y, (z + d // 2) % NZ, (core + d) % 2) for d in range(1, 2 * NZ)]
+    in_y = [device_at(x, (y + d) % NY, z, core) for d in range(1, NY)]
+    in_x = [device_at((x + d) % NX, y, z, core) for d in range(1, NX)]
+    return in_z, in_y, in_x
+
+
+def greet(targets, sem):
+    for target in targets:
+        pl.semaphore_signal(sem, inc=1, device_id=target, device_id_type=MESH)
 
 
 def front_row(r, i):
@@ -202,23 +215,29 @@
     r.update_t[i] = gating * projected
     d_proj_out = (upstream * gating).astype(jnp.bfloat16)
     r.d_proj_out[i] = d_proj_out
-    r.d_proj[i, pl.ds(512, 128)] = (upstream * projected * gating * (1.0 - gating)).astype(jnp.bfloat16)
+    r.d_gate[i] = (upstream * projected * gating * (1.0 - gating)).astype(jnp.bfloat16)
     d_xn = dot(r.out_w[...], d_proj_out, NN)
     r.out_scale[...] += d_xn * x_hat
     r.out_shift[...] += d_xn
     store_row(r.rows_b, i, standardize_back(d_xn * gain, x_hat, x_inv))
 
 
-def back_row(r, i):
-    mask = r.mask[pl.ds(i, 1)]
-    for t, rows in ((0, r.rows_a), (1, r.rows_b)):
-        d_factor = load_row(rows, i) * mask
-        value, sig = r.value[i, t], r.sig[i, t]
-        r.d_proj[i, pl.ds(t * 256, 128)] = (d_factor * sig).astype(jnp.bfloat16)
-        r.d_proj[i, pl.ds(t * 256 + 128, 128)] = (d_factor * value * sig * (1.0 - sig)).astype(jnp.bfloat16)
-    d_proj = r.d_proj[i]
-    r.part[pl.ds(0, 640)] += dot(d_proj, r.normed[i], NT)
-    d_normed = dot(r.proj_w[...], d_proj, NN)
+def back_row(r, i, t, rows):
+    d_factor = load_row(rows, i) * r.mask[pl.ds(i, 1)]
+    value, sig = r.value[i, t], r.sig[i, t]
+    d_value = (d_factor * sig).astype(jnp.bfloat16)
+    d_gate = (d_factor * value * sig * (1.0 - sig)).astype(jnp.bfloat16)
+    d_proj = jnp.concatenate([d_value, d_gate], axis=0)
+    r.part[pl.ds(t * 256, 256)] += dot(d_proj, r.normed[i], NT)
+    return r.d_normed[i] + dot(r.proj_w[:, t * 256 : t * 256 + 256], d_proj, NN)
+
+
+def left_row(r, i):
+    r.d_normed[i] = back_row(r, i, 0, r.rows_a)
+
+
+def right_row(r, i):
+    d_normed = back_row(r, i, 1, r.rows_b)
     r.d_normed[i] = d_normed
     r.in_scale[...] += d_normed * r.z_hat[i]
     r.in_shift[...] += d_normed
@@ -250,40 +269,83 @@
     return jnp.sum((value[:, :128] + value[:, 128:]).T, axis=0, keepdims=True)
 
 
-def start_factors(r):
-    row, rep = lax.axis_index("row"), lax.axis_index("rep")
-    over_rows(front_row, r)
-    r.send_f[:, 0] = to_tiles(r.rows_a)
-    r.send_f[:, 1] = to_tiles(r.rows_b)
-    place = r.recv_f.at[row // 64, :, rep * 64 + row % 64]
-    send_to_owners(r.send_f, place, r.sem.at[0], r.sem.at[1])
+def prepare(r):
+    row, rep = lax.axis_index("row"), lax.axis_index("rep")
+    r.proj_t[...] = r.proj_w[...].astype(jnp.float32).T.astype(jnp.bfloat16)
+    r.out_t[...] = r.out_w[...].astype(jnp.float32).T.astype(jnp.bfloat16)
+    for column, vector in (
+        (r.in_gain, r.in_gain_row), (r.in_bias, r.in_bias_row), (r.out_gain, r.out_gain_row), (r.out_bias, r.out_bias_row),
+    ):
+        column[...] = jnp.broadcast_to(vector[...], (128, 128)).T
+    cols = jnp.concatenate([r.mask_cols[pl.ds(rep * 2, 1)], r.mask_cols[pl.ds(rep * 2 + 1, 1)]], axis=1)
+    cols = cols.astype(jnp.float32)
+    for i in range(8):
+        r.mask[pl.ds(i, 1)] = cols * r.mask_rows[row * 8 + i].astype(jnp.float32)
+
+
+def enter(r):
+    in_z, in_y, in_x = neighbours()
+    barrier = pltpu.get_barrier_semaphore()
+    greet(in_z + in_y + in_x, barrier)
+    prepare(r)
+
+    def step(i, carry):
+        front_row(r, i)
+        return carry
+
+    lax.fori_loop(0, 4, step, 0)
+    pl.semaphore_wait(barrier, len(in_z) + len(in_y) + len(in_x))
+    greet(in_y, r.plane_sem)
+    lax.fori_loop(4, 8, step, 0)
+    pl.semaphore_wait(r.plane_sem, len(in_y))
+    greet(in_x, r.all_sem)
+    r.send_r[...] = to_tiles(r.rows_b)
+    r.send_l[...] = to_tiles(r.rows_a)
+    pl.semaphore_wait(r.all_sem, len(in_x))
+
+
+def swap_right(r):
+    row, rep = lax.axis_index("row"), lax.axis_index("rep")
+    mine = r.recv_r.at[row % 2]
+    return remote(mine, mine, r.sem.at[2], r.sem.at[3], (row + 1 - 2 * (row % 2), rep))
+
+
+def send_factors(r):
+    row, rep = lax.axis_index("row"), lax.axis_index("rep")
+    half, slot = row // 64, rep * 64 + row % 64
+    send_to_owners(r.send_r, r.recv_r.at[half, slot], r.sem.at[0], r.sem.at[1])
+    send_to_owners(r.send_l, r.recv_l.at[slot], r.sem.at[16], r.sem.at[17], 0, 32)
+
+    @pl.when((row // 32) % 2 == 0)
+    def _():
+        wait_for(r.recv_r.at[row % 2], r.sem.at[1])
+        swap_right(r).start()
+
+    send_to_owners(r.send_l, r.recv_l.at[slot], r.sem.at[16], r.sem.at[17], 32, 128)
 
 
 def own_product(r):
     x, y, z, core = coordinates()
-    row, rep = lax.axis_index("row"), lax.axis_index("rep")
-    wait_for(r.recv_f.at[core], r.sem.at[1])
-    mine = r.recv_f.at[core, 1]
-    swap = remote(mine, mine, r.sem.at[2], r.sem.at[3], (row + 1 - 2 * core, rep))
-    swap.start()
-
-    def build(half, k):
-        rows = pl.ds(aligned(half * 512, 512), 512)
-        slots = pl.ds(aligned(k * 64, 64), 64)
-        r.right[k, rows] = unpack(r.recv_f[half, 1, slots]).astype(jnp.bfloat16)
-
-    def own(k, carry):
-        r.left[k] = unpack(r.recv_f[core, 0, pl.ds(aligned(k * 64, 64), 64)]).astype(jnp.bfloat16)
-        build(core, k)
-        return carry
-
-    def other(k, carry):
-        build(1 - core, k)
-        return carry
-
-    lax.fori_loop(0, 4, own, 0)
-    swap.wait_recv()
-    lax.fori_loop(0, 4, other, 0)
+    rep = lax.axis_index("rep")
+
+    def build(half):
+        def step(k, carry):
+            rows = pl.ds(aligned(half * 512, 512), 512)
+            slots = pl.ds(aligned(k * 64, 64), 64)
+            r.right[k, rows] = unpack(r.recv_r[half, slots]).astype(jnp.bfloat16)
+            return carry
+
+        lax.fori_loop(0, 4, step, 0)
+
+    def build_left(k, carry):
+        r.left[k] = unpack(r.recv_l[pl.ds(aligned(k * 64, 64), 64)]).astype(jnp.bfloat16)
+        return carry
+
+    build(core)
+    swap_right(r).wait()
+    build(1 - core)
+    wait_for(r.recv_l, r.sem.at[17])
+    lax.fori_loop(0, 4, build_left, 0)
 
     def result(q, carry):
         part = turn(q, 1 - 2 * (x // 2), rep)
@@ -296,7 +358,6 @@
         return carry
 
     lax.fori_loop(0, 4, result, 0)
-    swap.wait_send()
     left_swap(r).start()
 
 
@@ -320,19 +381,20 @@
         return carry
 
     lax.fori_loop(0, 4, build, 0)
+    def for_left(q, carry):
+        part = turn(q, 1 - 2 * (x // 2), rep)
+        total = dot(r.d_own[0], r.right[part, pl.ds(0, 256)], NN)
+        for k in range(1, 4):
+            total += dot(r.d_own[k], r.right[part, pl.ds(k * 256, 256)], NN)
+        r.back_l[:, pl.ds(aligned(part * 32, 32), 32)] = pack(total)
+        start_hop(r.back_l, r.stage_l, part, r.sem.at[11], r.hop_l)
+        return carry
+
+    lax.fori_loop(0, 4, for_left, 0)
     for a in range(2):
         slots = pl.ds(aligned(core * 128 + a * 64, 64), 64)
         r.d_mine[a] = unpack(r.recv_d[slots]).T.astype(jnp.bfloat16)
-
-    def for_left(part, carry):
-        total = dot(r.d_own[0], r.right[part, pl.ds(0, 256)], NN)
-        for k in range(1, 4):
-            total += dot(r.d_own[k], r.right[part, pl.ds(k * 256, 256)], NN)
-        r.back_d[:, pl.ds(aligned(part * 32, 32), 32), 0] = pack(total)
-        return carry
-
-    lax.fori_loop(0, 4, for_left, 0)
-    crossing.wait_recv()
+    crossing.wait()
     for a in range(2):
         r.d_cross[a] = unpack(r.cross[pl.ds(a * 64, 64)]).T.astype(jnp.bfloat16)
     left_swap(r).wait()
@@ -342,12 +404,11 @@
         totals = [
             dot(r.d_mine[a], r.left[part], NN) + dot(r.d_cross[a], r.left_other[part], NN) for a in range(2)
         ]
-        r.back_d[:, pl.ds(aligned(part * 32, 32), 32), 1] = pack(jnp.concatenate(totals, axis=0))
-        start_hop(r.back_d, r.stage_d, part, r.sem.at[11], r.hop_d)
+        r.back_r[:, pl.ds(aligned(part * 32, 32), 32)] = pack(jnp.concatenate(totals, axis=0))
+        start_hop(r.back_r, r.stage_r, part, r.sem.at[18], r.hop_r)
         return carry
 
     lax.fori_loop(0, 4, for_right, 0)
-    crossing.wait_send()
 
 
 def sum_over_devices(r, meanwhile):
@@ -390,17 +451,19 @@
         ).start()
     wait_for(r.y_rows.at[pl.ds(0, NY - 1)], recvs.at[3])
 
-    r.z_rows[z] = r.y_rows[...]
+    r.z_part[...] = r.y_rows[...].reshape(64, 128).astype(jnp.bfloat16)
+    r.z_rows[z] = r.z_part[...]
     for dz in range(1, NZ):
         remote(
-            r.y_rows, r.z_rows.at[z], sends.at[4], recvs.at[4], device_at(x, y, (z + dz) % NZ, core)
+            r.z_part, r.z_rows.at[z], sends.at[4], recvs.at[4], device_at(x, y, (z + dz) % NZ, core)
         ).start()
     wait_for(r.z_rows.at[pl.ds(0, NZ - 1)], recvs.at[4])
 
-    r.sums[core] = r.z_rows[...]
-    last = remote(r.z_rows, r.sums.at[core], sends.at[5], recvs.at[5], sibling)
+    r.both[core] = r.z_rows[...]
+    last = remote(r.z_rows, r.both.at[core], sends.at[5], recvs.at[5], sibling)
     last.start()
     last.wait()
+    r.sums[...] = r.both[...].reshape(1024, 128).astype(jnp.float32) * (1.0 / r.mask_rows.shape[0])
 
     first.wait_send()
     wait_for(r.from_z.at[pl.ds(0, NZ - 1)], sends.at[1])
@@ -415,7 +478,8 @@
     row, rep = lax.axis_index("row"), lax.axis_index("rep")
     owner = x % 2 == 0
 
-    start_factors(r)
+    enter(r)
+    send_factors(r)
 
     def turn_cotangent(r, i):
         r.upstream[i] = r.cotangent[i].astype(jnp.float32).T
@@ -437,36 +501,44 @@
     r.send_d[...] = to_tiles(r.rows_b)
     send_to_owners(r.send_d, r.recv_d.at[rep * 64 + row % 64], r.sem.at[7], r.sem.at[8])
 
-    def finish_update(r, i):
+    def finish_middle(r, i):
         r.update[i] = r.update_t[i].T.astype(jnp.bfloat16)
+        d_gate = r.d_gate[i]
+        r.part[pl.ds(512, 128)] += dot(d_gate, r.normed[i], NT)
         r.part[pl.ds(640, 128)] += dot(r.xn[i], r.d_proj_out[i], NT)
-
-    over_rows(finish_update, r)
+        r.d_normed[i] = dot(r.proj_w[:, 512:], d_gate, NN)
+
+    over_rows(finish_middle, r)
 
     @pl.when(owner)
     def _():
         own_gradients(r)
 
-    spread(r.stage_d, r.recv_g, r.hop_d, r.sem.at[14], r.sem.at[15])
-    wait_for(r.recv_g, r.sem.at[15])
-
-    to_f32_rows(r.rows_a, r.recv_g[:, 0])
-    to_f32_rows(r.rows_b, r.recv_g[:, 1])
-    over_rows(back_row, r)
+    spread(r.stage_l, r.recv_gl, r.hop_l, r.sem.at[14], r.sem.at[15])
+    spread(r.stage_r, r.recv_gr, r.hop_r, r.sem.at[19], r.sem.at[20])
+    wait_for(r.recv_gl, r.sem.at[15])
+    to_f32_rows(r.rows_a, r.recv_gl[...])
+    over_rows(left_row, r)
+    wait_for(r.recv_gr, r.sem.at[20])
+    to_f32_rows(r.rows_b, r.recv_gr[...])
+    over_rows(right_row, r)
     norms = [channel_sums(ref[...]) for ref in (r.in_scale, r.in_shift, r.out_scale, r.out_shift)]
     r.part[pl.ds(768, 8)] = jnp.concatenate(norms + [jnp.zeros((4, 128), jnp.float32)], axis=0)
 
     sum_over_devices(r, lambda: over_rows(grad_row, r))
 
-    finish_sends(r.send_f, r.sem.at[0])
+    finish_sends(r.send_r, r.sem.at[0])
+    finish_sends(r.send_l, r.sem.at[16])
     finish_sends(r.send_d, r.sem.at[7])
     wait_for(r.stage_p.at[pl.ds(0, 127)], r.sem.at[12])
-    wait_for(r.stage_d.at[pl.ds(0, 127)], r.sem.at[14])
+    wait_for(r.stage_l.at[pl.ds(0, 127)], r.sem.at[14])
+    wait_for(r.stage_r.at[pl.ds(0, 127)], r.sem.at[19])
 
     @pl.when(owner)
     def _():
         finish_hop(r.back_p, r.sem.at[4])
-        finish_hop(r.back_d, r.sem.at[11])
+        finish_hop(r.back_l, r.sem.at[11])
+        finish_hop(r.back_r, r.sem.at[18])
 
 
 VMEM = pl.BlockSpec(memory_space=pltpu.VMEM)
@@ -492,14 +564,23 @@
         "xn": of(bf16, 8, 128, 256),
         "update_t": of(f32, 8, 128, 256),
         "d_proj_out": of(bf16, 8, 128, 256),
-        "d_proj": of(bf16, 8, 640, 256),
+        "d_gate": of(bf16, 8, 128, 256),
+        "mask": of(f32, 8, 256),
+        "in_gain": of(f32, 128, 128),
+        "in_bias": of(f32, 128, 128),
+        "out_gain": of(f32, 128, 128),
+        "out_bias": of(f32, 128, 128),
+        "proj_t": of(bf16, 640, 128),
+        "out_t": of(bf16, 128, 128),
         "d_normed": of(f32, 8, 128, 256),
         "out_scale": of(f32, 128, 256),
         "out_shift": of(f32, 128, 256),
         "in_scale": of(f32, 128, 256),
         "in_shift": of(f32, 128, 256),
-        "send_f": of(bf16, 128, 2, 16, 128),
-        "recv_f": of(bf16, 2, 2, 256, 16, 128),
+        "send_l": of(bf16, 128, 16, 128),
+        "send_r": of(bf16, 128, 16, 128),
+        "recv_l": of(bf16, 256, 16, 128),
+        "recv_r": of(bf16, 2, 256, 16, 128),
         "left": of(bf16, 4, 512, 256),
         "right": of(bf16, 4, 1024, 256),
         "back_p": of(bf16, 2, 128, 16, 128),
@@ -512,9 +593,12 @@
         "d_own": of(bf16, 4, 512, 256),
         "d_mine": of(bf16, 2, 256, 512),
         "d_cross": of(bf16, 2, 256, 512),
-        "back_d": of(bf16, 2, 128, 2, 16, 128),
-        "stage_d": of(bf16, 128, 2, 16, 128),
-        "recv_g": of(bf16, 128, 2, 16, 128),
+        "back_l": of(bf16, 2, 128, 16, 128),
+        "back_r": of(bf16, 2, 128, 16, 128),
+        "stage_l": of(bf16, 128, 16, 128),
+        "stage_r": of(bf16, 128, 16, 128),
+        "recv_gl": of(bf16, 128, 16, 128),
+        "recv_gr": of(bf16, 128, 16, 128),
         "part": of(f32, 1024, 128),
         "from_core": of(f32, 512, 128),
         "half": of(f32, 512, 128),
@@ -523,17 +607,23 @@
         "from_xy": of(f32, 32, 8, 128),
         "xy_sum": of(f32, 8, 128),
         "y_rows": of(f32, 8, 8, 128),
-        "z_rows": of(f32, 8, 8, 8, 128),
-        "sem": DMA((16,)),
+        "z_part": of(bf16, 64, 128),
+        "z_rows": of(bf16, 8, 64, 128),
+        "both": of(bf16, 2, 8, 64, 128),
+        "sem": DMA((21,)),
         "hop_p": DMA((4,)),
-        "hop_d": DMA((4,)),
+        "hop_l": DMA((4,)),
+        "hop_r": DMA((4,)),
+        "plane_sem": pltpu.SemaphoreType.REGULAR,
+        "all_sem": pltpu.SemaphoreType.REGULAR,
         "sum_send": DMA((6,)),
         "sum_recv": DMA((6,)),
     }
 
 
 INPUTS = (
-    "pair", "cotangent", "mask", "in_gain", "in_bias", "out_gain", "out_bias", "proj_w", "proj_t", "out_w", "out_t",
+    "mask_rows", "mask_cols", "pair", "cotangent", "in_gain_row", "in_bias_row", "out_gain_row", "out_bias_row",
+    "proj_w", "out_w",
 )
 OUTPUTS = ("update", "grad_pair", "sums")
 
@@ -544,11 +634,13 @@
     block = jax.ShapeDtypeStruct((8, 256, 128), jnp.bfloat16)
     return pl.pallas_call(
         functools.partial(step_kernel, names),
-        out_shape=(block, block, jax.ShapeDtypeStruct((2, 8, 8, 8, 128), jnp.float32)),
-        in_specs=[VMEM] * len(INPUTS),
+        out_shape=(block, block, jax.ShapeDtypeStruct((1024, 128), jnp.float32)),
+        in_specs=[pl.BlockSpec(memory_space=pltpu.SMEM)] + [VMEM] * (len(INPUTS) - 1),
         out_specs=(VMEM,) * 3,
         scratch_shapes=list(extra.values()),
-        compiler_params=pltpu.CompilerParams(has_side_effects=True, vmem_limit_bytes=56 << 20),
+        compiler_params=pltpu.CompilerParams(
+            has_side_effects=True, collective_id=0, vmem_limit_bytes=56 << 20
+        ),
         name="triangle_step",
     )(*args)
 
@@ -556,18 +648,15 @@
 def body(
     pair, cotangent, token_mask, in_gain, in_bias, proj_weight, out_gain, out_bias, out_weight
 ):
-    row_count, col_count, channels = pair.shape
-    mask_f = token_mask.astype(jnp.float32)
-    rows = lax.dynamic_slice_in_dim(mask_f, lax.axis_index("row") * row_count, row_count)
-    cols = lax.dynamic_slice_in_dim(mask_f, lax.axis_index("rep") * col_count, col_count)
-    vectors = [
-        jnp.broadcast_to(v[:, None], (channels, 128)) for v in (in_gain, in_bias, out_gain, out_bias)
-    ]
-    update, grad_pair, sums = whole_step(
-        pair, cotangent, rows[:, None] * cols[None, :], *vectors,
-        proj_weight, proj_weight.T, out_weight, out_weight.T,
+    update, grad_pair, total = whole_step(
+        token_mask,
+        token_mask.reshape(8, 128),
+        pair,
+        cotangent,
+        *[v.reshape(1, 128) for v in (in_gain, in_bias, out_gain, out_bias)],
+        proj_weight,
+        out_weight,
     )
-    total = sums.reshape(1024, 128) * (1.0 / token_mask.shape[0])
     return (update, grad_pair, total[:640].T, total[640:768], total[768:770], total[770:772])
 
 

time: 198 us -> 170 us (0.86)
  Pallas kernels: 186 us -> 162 us
  other arithmetic: 2.43 us -> 0 us
  local copies, waits for them, and re-layouts: 8.8 us -> 6.76 us
    pallas_call x1, Pallas kernels: 186 us -> 162 us  [whole_step(): pl.pallas_call(functools.partial(step_kernel, names), out_shape=(block, b...]
    broadcast_in_dim x4 -> x0, local copies, waits for them, and re-layouts: 2.84 us -> none  [body(): jnp.broadcast_to(v[:, None], (channels, 128))]
    unnamed x21 -> x7, local copies, waits for them, and re-layouts: 4.58 us -> 2.92 us
where the time goes in v2:
time: 170 us
  Pallas kernels  162 us (95%)
  local copies, waits for them, and re-layouts  6.76 us (4%)
    pallas_call x1, Pallas kernels, whole_step(): pl.pallas_call(functools.partial(step_kernel, names), out_shape=(block, b...  162 us

profile of v2, /device:TPU:1, one launch (start us, length us, event | category | flops | bytes accessed | tf_op | source)
XLA Modules:
  0.0 169.7 jit_solution(17961263306566649258)
XLA Ops:
  0.6 162.3 %triangle_step.1 = (bf16[8,256,128]{2,1,0:T(8,128)(2,1)}, bf16[8,256,128]{2,1,0:T(8,128)(2,1)}, f32[1024,128]{1,0:T(8,128)}) custom-call(s32[1024]{0:T(1024)} %refs_0_.1, s32[8,128]{1,0:T(8,128)} %bitcast.7, bf16[8,256,128]{2,1,0:T(8,128)(2,1)} %refs_2_.1, bf16[8,256,128]{2,1,0:T(8,128)(2,1)} %refs_3_.1, f32[1,128]{1,0:T(1,128)} %bitcast.8, ...), custom_call_target="tpu_custom_call" | custom-call | tf_op jit(solution)/shard_map/triangle_step/pallas_call | solution.py:635
  162.9 1.3 fusion
  164.3 1.5 slice.13
  165.7 0.0 copy-start.1
  165.7 1.1 slice_bitcast_fusion
  166.8 0.9 copy.15
  167.7 0.0 copy-done.1
  167.7 0.0 copy-start
  167.7 0.8 copy.18
  168.5 0.4 copy-done
  168.9 0.8 copy.19
Async XLA Ops:
  165.7 2.0 %copy-start.1 = (bf16[8,256,128]{2,1,0:T(8,128)(2,1)S(1)}, bf16[8,256,128]{2,1,0:T(8,128)(2,1)}, u32[]{:S(2)}) copy-start(bf16[8,256,128]{2,1,0:T(8,128)(2,1)} %get-tuple-element.26) | copy-start | bytes 1572868
  167.7 1.2 copy-start

commit v3 on v2

--- a/solution.py
+++ b/solution.py
@@ -96,49 +96,75 @@
     return (rep + sign * q + 4) % 4
 
 
+def way_back():
+    x, y, z, core = coordinates()
+    even = x % 2 == 0
+    hx = jnp.where(even, x // 2, core)
+    half = jnp.where(even, core, x // 2)
+    differ = (hx + half) % 2
+    plane = jnp.where(even, (x + 3 * differ) % 4, 2 * half + 1 - differ)
+    return hx, half, differ, plane
+
+
 def start_hop(send, stage, part, hop_send, hop_recv):
     x, y, z, core = coordinates()
-    me = (lax.axis_index("row"), lax.axis_index("rep"))
+    hx, half, differ, plane = way_back()
     rows = pl.ds(aligned(part * 32, 32), 32)
-    for bx in range(2):
-        target = device_at(2 * core + bx, y, z, x // 2)
-        copy_to(send.at[bx, rows], stage.at[rows], hop_send, hop_recv.at[part], target, me)
+    target = device_at((x + 1 + 2 * differ) % 4, y, z, hx)
+    other = 1 - (plane - 2 * half)
+    remote(send.at[other, rows], stage.at[rows], hop_send, hop_recv.at[part], target).start()
 
 
 def finish_hop(send, hop_send):
-    x, y, z, core = coordinates()
-
-    @pl.when(core == x // 2)
-    def _():
-        wait_for(send.at[0], hop_send)
-
-    @pl.when(core != x // 2)
-    def _():
-        wait_for(send, hop_send)
-
-
-def spread(stage, recv, hop_recv, send_sem, recv_sem):
+    wait_for(send.at[0], hop_send)
+
+
+def spread(send, stage, recv, hop_recv, send_sem, recv_sem):
     x, y, z, core = coordinates()
     rep = lax.axis_index("rep")
     me = (lax.axis_index("row"), rep)
-    h = core * 64 + y * 8 + z
+    hx, half, differ, plane = way_back()
+    h = hx * 64 + y * 8 + z
     sign = 1 - 2 * core
 
-    def one_part(q, carry):
-        part = turn(q, sign, rep)
-        wait_for(stage.at[pl.ds(aligned(part * 32, 32), 32)], hop_recv.at[part])
-
-        def step(s, carry):
-            tc, dz, dy = (s + core) % 2, (s // 2) % 8, s // 16
-            ty, tz = part * 2 + (y + dy) % 2, (z + sign * dz + 8) % 8
-            place = part * 32 + (ty % 2) * 16 + tz * 2 + tc
-            copy_to(stage.at[place], recv.at[h], send_sem, recv_sem, device_at(x, ty, tz, tc), me)
+    def all_parts(source, staged):
+        def one_part(q, carry):
+            part = turn(q, 1 - 2 * differ, rep)
+            if staged:
+                wait_for(source.at[pl.ds(aligned(part * 32, 32), 32)], hop_recv.at[part])
+
+            def step(s, carry):
+                tc, dz, dy = (s + core) % 2, (s // 2) % 8, s // 16
+                ty, tz = part * 2 + (y + dy) % 2, (z + sign * dz + 8) % 8
+                place = part * 32 + (ty % 2) * 16 + tz * 2 + tc
+                copy_to(source.at[place], recv.at[h], send_sem, recv_sem, device_at(plane, ty, tz, tc), me)
+                return carry
+
+            lax.fori_loop(0, 32, step, 0)
             return carry
 
-        lax.fori_loop(0, 32, step, 0)
-        return carry
-
-    lax.fori_loop(0, 4, one_part, 0)
+        lax.fori_loop(0, 4, one_part, 0)
+
+    @pl.when(x % 2 == 0)
+    def _():
+        all_parts(send.at[plane - 2 * half], False)
+
+    @pl.when(x % 2 == 1)
+    def _():
+        all_parts(stage, True)
+
+
+def finish_spread(stage, send_sem):
+    x, y, z, core = coordinates()
+    plane = way_back()[3]
+
+    @pl.when(plane == x)
+    def _():
+        wait_for(stage.at[pl.ds(0, 127)], send_sem)
+
+    @pl.when(plane != x)
+    def _():
+        wait_for(stage, send_sem)
 
 
 def rows_of(ref, row):
@@ -348,7 +374,7 @@
     lax.fori_loop(0, 4, build_left, 0)
 
     def result(q, carry):
-        part = turn(q, 1 - 2 * (x // 2), rep)
+        part = turn(q, 1 - 2 * ((x // 2 + core) % 2), rep)
         rows = pl.ds(aligned(part * 256, 256), 256)
         total = dot(r.left[0], r.right[0, rows], NT)
         for k in range(1, 4):
@@ -382,7 +408,7 @@
 
     lax.fori_loop(0, 4, build, 0)
     def for_left(q, carry):
-        part = turn(q, 1 - 2 * (x // 2), rep)
+        part = turn(q, 1 - 2 * ((x // 2 + core) % 2), rep)
         total = dot(r.d_own[0], r.right[part, pl.ds(0, 256)], NN)
         for k in range(1, 4):
             total += dot(r.d_own[k], r.right[part, pl.ds(k * 256, 256)], NN)
@@ -400,7 +426,7 @@
     left_swap(r).wait()
 
     def for_right(q, carry):
-        part = turn(q, 1 - 2 * (x // 2), rep)
+        part = turn(q, 1 - 2 * ((x // 2 + core) % 2), rep)
         totals = [
             dot(r.d_mine[a], r.left[part], NN) + dot(r.d_cross[a], r.left_other[part], NN) for a in range(2)
         ]
@@ -463,7 +489,12 @@
     last = remote(r.z_rows, r.both.at[core], sends.at[5], recvs.at[5], sibling)
     last.start()
     last.wait()
-    r.sums[...] = r.both[...].reshape(1024, 128).astype(jnp.float32) * (1.0 / r.mask_rows.shape[0])
+    total = r.both[...].reshape(1024, 128).astype(jnp.float32) * (1.0 / r.mask_rows.shape[0])
+    for b in range(5):
+        r.grad_proj[:, b * 128 : (b + 1) * 128] = total[b * 128 : (b + 1) * 128].T
+    r.grad_out[...] = total[640:768]
+    r.grad_in_norm[...] = total[768:770]
+    r.grad_out_norm[...] = total[770:772]
 
     first.wait_send()
     wait_for(r.from_z.at[pl.ds(0, NZ - 1)], sends.at[1])
@@ -493,7 +524,7 @@
     def _():
         own_product(r)
 
-    spread(r.stage_p, r.recv_p, r.hop_p, r.sem.at[12], r.sem.at[13])
+    spread(r.back_p, r.stage_p, r.recv_p, r.hop_p, r.sem.at[12], r.sem.at[13])
     wait_for(r.recv_p, r.sem.at[13])
 
     to_f32_rows(r.rows_a, r.recv_p[...])
@@ -514,8 +545,8 @@
     def _():
         own_gradients(r)
 
-    spread(r.stage_l, r.recv_gl, r.hop_l, r.sem.at[14], r.sem.at[15])
-    spread(r.stage_r, r.recv_gr, r.hop_r, r.sem.at[19], r.sem.at[20])
+    spread(r.back_l, r.stage_l, r.recv_gl, r.hop_l, r.sem.at[14], r.sem.at[15])
+    spread(r.back_r, r.stage_r, r.recv_gr, r.hop_r, r.sem.at[19], r.sem.at[20])
     wait_for(r.recv_gl, r.sem.at[15])
     to_f32_rows(r.rows_a, r.recv_gl[...])
     over_rows(left_row, r)
@@ -530,9 +561,9 @@
     finish_sends(r.send_r, r.sem.at[0])
     finish_sends(r.send_l, r.sem.at[16])
     finish_sends(r.send_d, r.sem.at[7])
-    wait_for(r.stage_p.at[pl.ds(0, 127)], r.sem.at[12])
-    wait_for(r.stage_l.at[pl.ds(0, 127)], r.sem.at[14])
-    wait_for(r.stage_r.at[pl.ds(0, 127)], r.sem.at[19])
+    finish_spread(r.stage_p, r.sem.at[12])
+    finish_spread(r.stage_l, r.sem.at[14])
+    finish_spread(r.stage_r, r.sem.at[19])
 
     @pl.when(owner)
     def _():
@@ -625,18 +656,22 @@
     "mask_rows", "mask_cols", "pair", "cotangent", "in_gain_row", "in_bias_row", "out_gain_row", "out_bias_row",
     "proj_w", "out_w",
 )
-OUTPUTS = ("update", "grad_pair", "sums")
+OUTPUTS = ("update", "grad_pair", "grad_proj", "grad_out", "grad_in_norm", "grad_out_norm")
 
 
 def whole_step(*args):
     extra = scratch()
     names = INPUTS + OUTPUTS + tuple(extra)
     block = jax.ShapeDtypeStruct((8, 256, 128), jnp.bfloat16)
+
+    def weights(*shape):
+        return jax.ShapeDtypeStruct(shape, jnp.float32)
+
     return pl.pallas_call(
         functools.partial(step_kernel, names),
-        out_shape=(block, block, jax.ShapeDtypeStruct((1024, 128), jnp.float32)),
+        out_shape=(block, block, weights(128, 640), weights(128, 128), weights(2, 128), weights(2, 128)),
         in_specs=[pl.BlockSpec(memory_space=pltpu.SMEM)] + [VMEM] * (len(INPUTS) - 1),
-        out_specs=(VMEM,) * 3,
+        out_specs=(VMEM,) * len(OUTPUTS),
         scratch_shapes=list(extra.values()),
         compiler_params=pltpu.CompilerParams(
             has_side_effects=True, collective_id=0, vmem_limit_bytes=56 << 20
@@ -648,7 +683,7 @@
 def body(
     pair, cotangent, token_mask, in_gain, in_bias, proj_weight, out_gain, out_bias, out_weight
 ):
-    update, grad_pair, total = whole_step(
+    return whole_step(
         token_mask,
         token_mask.reshape(8, 128),
         pair,
@@ -657,7 +692,6 @@
         proj_weight,
         out_weight,
     )
-    return (update, grad_pair, total[:640].T, total[640:768], total[768:770], total[770:772])
 
 
 def solution(mesh):

time: 170 us -> 167 us (0.982)
  Pallas kernels: 162 us -> 160 us
    unnamed x7 -> x16, local copies, waits for them, and re-layouts: 2.92 us -> 5.81 us
    slice x2 -> x0, local copies, waits for them, and re-layouts: 2.79 us -> none  [the longest x1 1.47 us: body(): total[640:768]]
    pallas_call x1, Pallas kernels: 162 us -> 160 us  [whole_step(): pl.pallas_call(functools.partial(step_kernel, names), out_shape=(block, b...]
where the time goes in v3:
time: 167 us
  Pallas kernels  160 us (96%)
  local copies, waits for them, and re-layouts  5.81 us (3%)
    pallas_call x1, Pallas kernels, whole_step(): pl.pallas_call(functools.partial(step_kernel, names), out_shape=(block, b...  160 us
    unnamed x16, local copies, waits for them, and re-layouts  5.81 us

profile of v3, /device:TPU:1, one launch (start us, length us, event | category | flops | bytes accessed | tf_op | source)
XLA Modules:
  0.0 166.8 jit_solution(17655748416895022690)
XLA Ops:
  0.6 160.4 %triangle_step.1 = (bf16[8,256,128]{2,1,0:T(8,128)(2,1)}, bf16[8,256,128]{2,1,0:T(8,128)(2,1)}, f32[128,640]{1,0:T(8,128)}, f32[128,128]{1,0:T(8,128)}, f32[2,128]{1,0:T(2,128)}, /*index=5*/f32[2,128]{1,0:T(2,128)}) custom-call(s32[1024]{0:T(1024)} %refs_0_.1, s32[8,128]{1,0:T(8,128)} %bitcast.5, bf16[8,256,128]{2,1,0:T(8,128)(2,1)} %refs_2_.1, ...), custom_call_target="tpu_custom_call" | custom-call | tf_op jit(solution)/shard_map/triangle_step/pallas_call | solution.py:670
  161.0 0.0 copy-start
  161.0 1.9 %copy.21 = bf16[8,256,128]{2,1,0:T(8,128)(2,1)} copy(bf16[8,256,128]{2,1,0:T(8,128)(2,1)} %get-tuple-element.12) | data formatting | bytes 1048576
  163.0 0.0 copy-done
  163.0 0.0 copy-start.1
  163.0 0.8 copy.22
  163.7 0.4 copy-done.1
  164.1 0.0 copy-start.2
  164.1 0.7 copy.23
  164.8 0.1 copy-done.2
  165.0 0.0 copy-start.4
  165.0 0.6 copy.24
  165.6 0.0 copy-done.4
  165.6 0.0 copy-start.3
  165.6 0.6 copy.25
  166.2 0.1 copy-done.3
  166.3 0.6 copy.26
Async XLA Ops:
  161.0 1.9 %copy-start = (bf16[8,256,128]{2,1,0:T(8,128)(2,1)S(1)}, bf16[8,256,128]{2,1,0:T(8,128)(2,1)}, u32[]{:S(2)}) copy-start(bf16[8,256,128]{2,1,0:T(8,128)(2,1)} %get-tuple-element.13) | copy-start | bytes 1572868
  163.0 1.2 copy-start.1
  164.1 0.9 copy-start.2
  165.0 0.6 copy-start.4
  165.6 0.7 copy-start.3

commit v4 on v3

--- a/solution.py
+++ b/solution.py
@@ -119,7 +119,7 @@
     wait_for(send.at[0], hop_send)
 
 
-def spread(send, stage, recv, hop_recv, send_sem, recv_sem):
+def spread(send, stage, recv, hop_recv, send_sem, recv_sem, in_turns=True):
     x, y, z, core = coordinates()
     rep = lax.axis_index("rep")
     me = (lax.axis_index("row"), rep)
@@ -145,13 +145,32 @@
 
         lax.fori_loop(0, 4, one_part, 0)
 
+    def at_once(source):
+        def step(s, carry):
+            tc, dy, dz = (s // 64 + core) % 2, (s // 8) % 8, s % 8
+            ty, tz = (y + sign * dy + 8) % 8, (z + sign * dz + 8) % 8
+            place = ty * 16 + tz * 2 + tc
+            copy_to(source.at[place], recv.at[h], send_sem, recv_sem, device_at(plane, ty, tz, tc), me)
+            return carry
+
+        lax.fori_loop(0, 128, step, 0)
+
     @pl.when(x % 2 == 0)
     def _():
-        all_parts(send.at[plane - 2 * half], False)
+        source = send.at[plane - 2 * half]
+        if in_turns:
+            all_parts(source, False)
+        else:
+            at_once(source)
 
     @pl.when(x % 2 == 1)
     def _():
-        all_parts(stage, True)
+        if in_turns:
+            all_parts(stage, True)
+        else:
+            for part in range(4):
+                wait_for(stage.at[pl.ds(part * 32, 32)], hop_recv.at[part])
+            at_once(stage)
 
 
 def finish_spread(stage, send_sem):
@@ -546,7 +565,7 @@
         own_gradients(r)
 
     spread(r.back_l, r.stage_l, r.recv_gl, r.hop_l, r.sem.at[14], r.sem.at[15])
-    spread(r.back_r, r.stage_r, r.recv_gr, r.hop_r, r.sem.at[19], r.sem.at[20])
+    spread(r.back_r, r.stage_r, r.recv_gr, r.hop_r, r.sem.at[19], r.sem.at[20], in_turns=False)
     wait_for(r.recv_gl, r.sem.at[15])
     to_f32_rows(r.rows_a, r.recv_gl[...])
     over_rows(left_row, r)

time: 167 us -> 166 us (level)
  no operation moved by 1% of the time
where the time goes in v4:
time: 166 us; the launch traced here: 165 us
  Pallas kernels  159 us (96%)
  local copies, waits for them, and re-layouts  5.81 us (4%)
    pallas_call x1, Pallas kernels, whole_step(): pl.pallas_call(functools.partial(step_kernel, names), out_shape=(block, b...  159 us
    unnamed x16, local copies, waits for them, and re-layouts  5.81 us

profile of v4, /device:TPU:1, one launch (start us, length us, event | category | flops | bytes accessed | tf_op | source)
XLA Modules:
  0.0 165.5 jit_solution(15983167365101670834)
XLA Ops:
  0.6 159.0 %triangle_step.1 = (bf16[8,256,128]{2,1,0:T(8,128)(2,1)}, bf16[8,256,128]{2,1,0:T(8,128)(2,1)}, f32[128,640]{1,0:T(8,128)}, f32[128,128]{1,0:T(8,128)}, f32[2,128]{1,0:T(2,128)}, /*index=5*/f32[2,128]{1,0:T(2,128)}) custom-call(s32[1024]{0:T(1024)} %refs_0_.1, s32[8,128]{1,0:T(8,128)} %bitcast.5, bf16[8,256,128]{2,1,0:T(8,128)(2,1)} %refs_2_.1, ...), custom_call_target="tpu_custom_call" | custom-call | tf_op jit(solution)/shard_map/triangle_step/pallas_call | solution.py:689
  159.6 0.0 copy-start
  159.6 1.9 %copy.21 = bf16[8,256,128]{2,1,0:T(8,128)(2,1)} copy(bf16[8,256,128]{2,1,0:T(8,128)(2,1)} %get-tuple-element.12) | data formatting | bytes 1048576
  161.6 0.0 copy-done
  161.6 0.0 copy-start.1
  161.6 0.8 copy.22
  162.4 0.4 copy-done.1
  162.7 0.0 copy-start.2
  162.7 0.7 copy.23
  163.5 0.1 copy-done.2
  163.6 0.0 copy-start.4
  163.6 0.6 copy.24
  164.2 0.0 copy-done.4
  164.2 0.0 copy-start.3
  164.2 0.6 copy.25
  164.8 0.1 copy-done.3
  164.9 0.6 copy.26
Async XLA Ops:
  159.6 1.9 %copy-start = (bf16[8,256,128]{2,1,0:T(8,128)(2,1)S(1)}, bf16[8,256,128]{2,1,0:T(8,128)(2,1)}, u32[]{:S(2)}) copy-start(bf16[8,256,128]{2,1,0:T(8,128)(2,1)} %get-tuple-element.13) | copy-start | bytes 1572868
  161.6 1.2 copy-start.1
  162.7 0.9 copy-start.2
  163.6 0.6 copy-start.4
  164.2 0.7 copy-start.3
